TPU v7x, 32 devices: a whole 2x2x4 slice. The times are simulated.
32 devices in a mesh: chan: 8 (over z, x), tile: 4 (over y, core).
Axes of the slice: x: 2, y: 2, z: 4, core: 2. Of those that a mesh axis runs over, the one named last changes fastest.
Arguments:
- voltages: bfloat16 [2, 1024, 5888], P(None, 'chan'), may hold values from -6 to 6
- taps: float32 [16, 256], replicated, may hold values from -0.09375 to 0.09375
- beam_weights: bfloat16 [2, 256, 64, 1024], P(None, 'chan'), may hold values from -0.1875 to 0.1875
- station_masks: int32 [64, 512], replicated, may hold values 0 or 1
- tile_pairs: int32 [36, 2], P('tile'), may hold values from 0 to 7, as said below
Outputs:
- visibilities: float32 [2, 256, 36, 128, 128], P(None, 'chan', 'tile')
- beams: bfloat16 [2, 64, 8, 256], P(None, 'tile', 'chan')
Inputs may be any that keep to these rules, and one draw needn't show every extreme that they name: `tile_pairs`: each pair (r, s) with 0 <= s <= r < 8 stands in exactly one row, r in the first column and s in the second.
All inputs are finite; a program needn't handle non-finite values.
Results may differ from a plain program's by a relative error of at most 0.0049.
Values may be sent and summed in bfloat16 or wider, within the bound.
A program may use at most 128 MiB of HBM per device.

v0:
```python
import math
import jax
import jax.numpy as jnp
from jax import lax
from jax.sharding import PartitionSpec as P

TB = 128


def dft_table(channels):
    counter = jnp.arange(channels, dtype=jnp.int32)
    wrapped = counter[:, None] * counter[None, :] % channels
    phases = 2.0 * math.pi / channels * wrapped.astype(jnp.float32)
    cosine = jnp.cos(phases)
    sine_part = jnp.sin(phases)
    first_row = jnp.stack([cosine, sine_part], axis=1)
    second_row = jnp.stack([-sine_part, cosine], axis=1)
    return jnp.stack([first_row, second_row], axis=1)


def filterbank(voltages, taps, count):
    taps_count, channels = taps.shape
    in_dev = voltages.shape[1]
    framed = voltages.reshape(2, in_dev, count + taps_count - 1, channels)
    frames = jnp.zeros((2, in_dev, count, channels), jnp.float32)
    for tap_index in range(taps_count):
        frames = frames + taps[tap_index] * framed[:, :, tap_index : tap_index + count, :].astype(
            jnp.float32
        )
    spectra = jnp.einsum(
        "crsk,sitk->crit",
        dft_table(channels),
        frames,
        precision=lax.Precision.HIGHEST,
        preferred_element_type=jnp.float32,
    )
    return spectra.astype(jnp.bfloat16)


def correlate(time_piece, tile_pairs):
    chan_dev = time_piece.shape[0]
    inputs = time_piece.shape[2]
    time_width = time_piece.shape[3]
    blocks = time_piece.reshape(chan_dev, 2, inputs // TB, TB, time_width)
    left_rows = jnp.take(blocks, tile_pairs[:, 0], axis=2)
    right_rows = jnp.take(blocks, tile_pairs[:, 1], axis=2)
    rotated = jnp.stack([left_rows[:, 1], -left_rows[:, 0]], axis=1)
    stacked = jnp.stack([left_rows, rotated], axis=0)
    return jnp.einsum(
        "ocrkaw,crkbw->ockab", stacked, right_rows, preferred_element_type=jnp.float32
    )


def beamform(own_time, beam_weights, station_masks):
    beams_count, stations = station_masks.shape
    live_inputs = jnp.broadcast_to(station_masks[:, :, None], (beams_count, stations, 2))
    live_inputs = live_inputs.reshape(beams_count, 2 * stations).astype(jnp.bfloat16)
    weights = beam_weights * live_inputs[None, None]
    products = jnp.einsum("scbi,crit->csrbt", weights, own_time, preferred_element_type=jnp.float32)
    real_part = products[:, 0, 0] - products[:, 1, 1]
    imag_part = products[:, 0, 1] + products[:, 1, 0]
    return jnp.transpose(jnp.stack([real_part, imag_part]), (0, 2, 3, 1)).astype(jnp.bfloat16)


def on_device(voltages, taps, beam_weights, station_masks, tile_pairs):
    taps_count, channels = taps.shape
    tile_count = lax.axis_size("tile")
    total_time = voltages.shape[2] // channels - taps_count + 1
    quarter = total_time // tile_count
    tile_index = lax.axis_index("tile")
    spectra = filterbank(voltages, taps, total_time)
    turned = lax.all_to_all(spectra, "chan", split_axis=0, concat_axis=2, tiled=True)
    own_time = lax.dynamic_slice_in_dim(turned, tile_index * quarter, quarter, 3)
    visibility = correlate(turned, tile_pairs)
    visibility = visibility * (1.0 / total_time)
    beam_part = beamform(own_time, beam_weights, station_masks)
    beams = lax.all_to_all(
        lax.all_to_all(beam_part, "tile", split_axis=1, concat_axis=2, tiled=True),
        "chan",
        split_axis=2,
        concat_axis=3,
        tiled=True,
    )
    return (visibility, beams)


def solution(mesh):
    in_specs = (P(None, "chan", None), P(), P(None, "chan", None, None), P(), P("tile", None))
    out_specs = (P(None, "chan", "tile", None, None), P(None, "tile", "chan", None))
    return jax.shard_map(
        on_device, mesh=mesh, in_specs=in_specs, out_specs=out_specs, check_vma=False
    )
```

profile of v0, /device:TPU:0, one launch (start us, length us, event | category | flops | bytes accessed | tf_op | source)
XLA Modules:
  0.0 124.9 jit_solution(12216933234083120169)
XLA Ops:
  0.6 1.0 fusion.109
  1.6 1.7 %fusion.107 = (f32[256,1,256]{2,0,1:T(8,128)S(1)}, f32[256,1,256]{2,0,1:T(8,128)}) fusion(), kind=kLoop, calls=%fused_computation.119 | loop fusion | flops 917504 | bytes 524288 | tf_op jit(solution)/shard_map/sin | solution.py:15
  3.3 1.7 %fusion.119 = (f32[1,256]{1,0:T(1,128)S(1)}, f32[1,256]{1,0:T(1,128)S(1)}, f32[1,256]{1,0:T(1,128)S(1)}, f32[1,256]{1,0:T(1,128)S(1)}, f32[1,256]{1,0:T(1,128)},...) fusion(f32[16,256]{1,0:T(8,128)} %param.8), kind=kLoop, calls=%fused_computation.141 | loop fusion | bytes 32768 | tf_op jit(solution)/shard_map/slice | solution.py:27
  5.0 3.5 %copy.96 = bf16[2,128,5888]{1,2,0:T(8,128)(2,1)S(1)} copy(bf16[2,128,5888]{2,1,0:T(8,128)(2,1)} %param.7) | data formatting | bytes 6029312 | tf_op args[0]
  8.5 1.1 maximum_bitcast_fusion.1
  9.6 7.1 %bitcast_convert_fusion = bf16[256,2,128,8]{2,0,3,1:T(8,128)(2,1)S(1)} fusion(bf16[2,128,23,256]{1,3,2,0:T(8,128)(2,1)S(1)} %bitcast.122, f32[256,1,2,256]{3,0,2,1:T(8,128)S(1)} %get-tuple-element.26, f32[256,1,2,256]{3,0,2,1:T(8,128)S(1)} %get-tuple-element.25, f32[256]{0:T(256)} %bitcast.145, f32[256]{0:T(256)} %bitcast.146, f32[256]{0:T(256)S(1)} %bitcast.132, ...), kind=kOutput, calls=%fused_computation.10 | convolution fusion | flops 3246653440 | bytes 18890752 | tf_op jit(solution)/shard_map/crsk,sitk->crit/dot_general | solution.py:30
  16.7 0.0 copy-start
  16.7 1.6 %copy.98 = bf16[256,2,128,8]{2,3,1,0:T(8,128)(2,1)} copy(bf16[256,2,128,8]{2,0,3,1:T(8,128)(2,1)S(1)} %bitcast_convert_fusion) | data formatting | bytes 2097152 | tf_op jit(solution)/shard_map/convert_element_type | solution.py:37
  18.4 0.0 copy-start.1
  18.4 7.4 %all-to-all-start = ((bf16[256,2,128,8]{2,3,1,0:T(8,128)(2,1)}), bf16[256,2,128,8]{2,3,1,0:T(8,128)(2,1)S(1)}, u32[]{:S(2)}, u32[]{:S(2)}) async-start(bf16[256,2,128,8]{2,3,1,0:T(8,128)(2,1)} %copy.98), calls=%async_computation | async-start | bytes 2097152 | tf_op jit(solution)/shard_map/all_to_all | solution.py:72
  25.8 0.0 copy-done
  25.8 0.1 copy.103
  25.9 0.1 broadcast_in_dim.11
  26.1 0.1 copy.104
  26.2 0.0 copy-done.1
  26.2 25.3 %all-to-all-done = bf16[256,2,128,8]{2,3,1,0:T(8,128)(2,1)S(1)} async-done(((bf16[256,2,128,8]{2,3,1,0:T(8,128)(2,1)}), bf16[256,2,128,8]{2,3,1,0:T(8,128)(2,1)S(1)}, u32[]{:S(2)}, u32[]{:S(2)}) %all-to-all-start) | async-done | bytes 1048608 | tf_op jit(solution)/shard_map/all_to_all | solution.py:72
  51.5 0.3 copy.144
  51.8 6.9 %fusion.58 = f32[32,2,2,64,2]{3,4,1,2,0:T(2,128)S(1)} fusion(bf16[32,2,1024,8]{2,3,1,0:T(8,128)(2,1)S(1)} %bitcast.118, s32[]{:T(128)S(6)} %select_n.39, bf16[2,32,64,1024]{3,2,1,0:T(8,128)(2,1)} %param.9, bf16[64,1024]{1,0:T(8,128)(2,1)S(1)} %copy.104), kind=kOutput, calls=%fused_computation.64 | convolution fusion | flops 37748736 | bytes 8847364 | tf_op jit(solution)/shard_map/scbi,crit->csrbt/dot_general | solution.py:59
  58.7 0.1 maximum_bitcast_fusion.3
  58.8 0.1 copy.108
  58.9 0.7 reshape.184
  59.7 3.3 %all-to-all-start.1 = ((bf16[4,2,1024]{2,1,0:T(2,128)(2,1)}), bf16[4,2,1024]{2,1,0:T(2,128)(2,1)S(1)}, u32[]{:S(2)}, u32[]{:S(2)}) async-start(bf16[4,2,1024]{2,1,0:T(2,128)(2,1)} %reshape.184), calls=%async_computation.1 | async-start | bytes 32768 | tf_op jit(solution)/shard_map/all_to_all | solution.py:78
  62.9 1.0 gather_fusion.1
  63.9 1.2 fusion.97
  65.1 0.2 fusion.118
  65.3 0.2 maximum_bitcast_fusion
  65.5 1.0 gather_fusion
  66.5 0.2 all-to-all-done.1
  66.7 0.1 reshape.185
  66.9 0.7 reshape.186
  67.6 3.6 %all-to-all-start.2 = ((bf16[8,2,512]{2,1,0:T(2,128)(2,1)}), bf16[8,2,512]{2,1,0:T(2,128)(2,1)S(1)}, u32[]{:S(2)}, u32[]{:S(2)}) async-start(bf16[8,2,512]{2,1,0:T(2,128)(2,1)} %reshape.186), calls=%async_computation.2 | async-start | bytes 32768 | tf_op jit(solution)/shard_map/all_to_all | solution.py:77
  71.2 16.0 %fusion = f32[2,32,9,128,128]{3,4,0,2,1:T(8,128)} fusion(bf16[1,32,2,9,128,8]{4,5,2,0,3,1:T(8,128)(2,1)S(1)} %maximum_bitcast_fusion, bf16[1,32,2,9,128,8]{4,5,2,0,3,1:T(8,128)(2,1)} %get-tuple-element.19, bf16[9,32,2,128,8]{3,4,2,1,0:T(8,128)(2,1)S(1)} %gather_fusion, pred[9]{0:T(512)(128)(4,1)S(1)} %get-tuple-element.15), kind=kOutput, calls=%fused_computation.3 | convolution fusion | flops 316735488 | bytes 41287688 | tf_op jit(solution)/shard_map/ocrkaw,crkbw->ockab/dot_general | solution.py:49
  87.2 36.9 %copy.113 = f32[2,32,9,128,128]{4,3,2,1,0:T(8,128)} copy(f32[2,32,9,128,128]{3,4,0,2,1:T(8,128)} %fusion) | data formatting | bytes 75497472
  124.1 0.0 all-to-all-done.2
  124.1 0.1 reshape.187
  124.2 0.7 all_to_all.44
  (9 shorter events, 0.1 us)
Async XLA Ops:
  16.7 9.1 %copy-start = (s32[64,512]{1,0:T(8,128)S(1)}, s32[64,512]{1,0:T(8,128)}, u32[]{:S(2)}) copy-start(s32[64,512]{1,0:T(8,128)} %param.10) | copy-start | bytes 393220
  18.4 7.8 %copy-start.1 = (s32[9,2]{0,1:T(2,128)S(1)}, s32[9,2]{0,1:T(2,128)}, u32[]{:S(2)}) copy-start(s32[9,2]{0,1:T(2,128)} %param.11) | copy-start | bytes 220
  18.4 33.2 %all-to-all-start = ((bf16[256,2,128,8]{2,3,1,0:T(8,128)(2,1)}), bf16[256,2,128,8]{2,3,1,0:T(8,128)(2,1)S(1)}, u32[]{:S(2)}, u32[]{:S(2)}) async-start(bf16[256,2,128,8]{2,3,1,0:T(8,128)(2,1)} %copy.98), calls=%async_computation | async-start | bytes 2097152 | tf_op jit(solution)/shard_map/all_to_all | solution.py:72
  59.7 7.1 %all-to-all-start.1 = ((bf16[4,2,1024]{2,1,0:T(2,128)(2,1)}), bf16[4,2,1024]{2,1,0:T(2,128)(2,1)S(1)}, u32[]{:S(2)}, u32[]{:S(2)}) async-start(bf16[4,2,1024]{2,1,0:T(2,128)(2,1)} %reshape.184), calls=%async_computation.1 | async-start | bytes 32768 | tf_op jit(solution)/shard_map/all_to_all | solution.py:78
  67.6 56.5 %all-to-all-start.2 = ((bf16[8,2,512]{2,1,0:T(2,128)(2,1)}), bf16[8,2,512]{2,1,0:T(2,128)(2,1)S(1)}, u32[]{:S(2)}, u32[]{:S(2)}) async-start(bf16[8,2,512]{2,1,0:T(2,128)(2,1)} %reshape.186), calls=%async_computation.2 | async-start | bytes 32768 | tf_op jit(solution)/shard_map/all_to_all | solution.py:77
where the time goes:
time: 126 us; the launch traced here: 125 us
  local copies, waits for them, and re-layouts  48.9 us (39%)
  matrix products  29.9 us (24%)
  waiting for transfers between devices  25.5 us (20%)
  starting transfers between devices  14.2 us (11%)
  other arithmetic  5.54 us (4%)
    unnamed x10, local copies, waits for them, and re-layouts  42 us
    all_to_all x1, waiting for transfers between devices, on_device(): lax.all_to_all(spectra, 'chan', split_axis=0, concat_axis=2, tiled=True)  25.3 us
    dot_general x1, matrix products, correlate(): jnp.einsum('ocrkaw,crkbw->ockab', stacked, right_rows, preferred_element_...  16 us
    all_to_all x1, starting transfers between devices, on_device(): lax.all_to_all(spectra, 'chan', split_axis=0, concat_axis=2, tiled=True)  7.38 us
    dot_general x1, matrix products, filterbank(): jnp.einsum('crsk,sitk->crit', dft_table(channels), frames, precision=lax....  7.12 us
    dot_general x1, matrix products, beamform(): jnp.einsum('scbi,crit->csrbt', weights, own_time, preferred_element_type=...  6.86 us
    all_to_all x1, starting transfers between devices, on_device(): lax.all_to_all(lax.all_to_all(beam_part, 'tile', split_axis=1, concat_axi...  3.59 us
    all_to_all x1, starting transfers between devices, on_device(): lax.all_to_all(beam_part, 'tile', split_axis=1, concat_axis=2, tiled=True)  3.25 us
  transfers between devices with their start and end apart: 3, of which 2 were waited for; matrix products, arithmetic and copies ran while one was open for 46% of the time, Pallas kernels for 0%

commit v1 on v0

--- a/solution.py
+++ b/solution.py
@@ -3,6 +3,7 @@
 import jax.numpy as jnp
 from jax import lax
 from jax.sharding import PartitionSpec as P
+from jax.lax import axis_index, axis_size, ppermute
 
 TB = 128
 
@@ -69,7 +70,27 @@
     quarter = total_time // tile_count
     tile_index = lax.axis_index("tile")
     spectra = filterbank(voltages, taps, total_time)
-    turned = lax.all_to_all(spectra, "chan", split_axis=0, concat_axis=2, tiled=True)
+    kept_arr = axis_size("chan")
+    view_out, w_next = (kept_arr, axis_index("chan"))
+    next_value = spectra.shape[0] // view_out
+    piece_now = list(spectra.shape)
+    piece_now[0] = next_value
+    everything = piece_now[2]
+    piece_now[2] = everything * view_out
+    turned = jnp.zeros(piece_now, spectra.dtype)
+    ii = 0
+    while ii < view_out:
+        carry_out = lax.dynamic_slice_in_dim(
+            spectra, (w_next ^ ii) * next_value, next_value, axis=0
+        )
+        if ii:
+            carry_out = ppermute(
+                carry_out, axis_name="chan", perm=[(dev_i, dev_i ^ ii) for dev_i in range(view_out)]
+            )
+        turned = lax.dynamic_update_slice_in_dim(
+            turned, carry_out, (w_next ^ ii) * everything, axis=2
+        )
+        ii += 1
     own_time = lax.dynamic_slice_in_dim(turned, tile_index * quarter, quarter, 3)
     visibility = correlate(turned, tile_pairs)
     visibility = visibility * (1.0 / total_time)

time: 126 us -> 122 us (0.968)
  waiting for transfers between devices: 25.5 us -> 12.5 us
  starting transfers between devices: 14.2 us -> 24.5 us
    all_to_all x1 -> x0, waiting for transfers between devices: 25.3 us -> none  [on_device(): lax.all_to_all(spectra, 'chan', split_axis=0, concat_axis=2, tiled=True)]
    ppermute x0 -> x7, starting transfers between devices: none -> 17.1 us  [on_device(): ppermute(carry_out, axis_name='chan', perm=[(dev_i, dev_i ^ ii) for dev_i...]
    ppermute x0 -> x7, waiting for transfers between devices: none -> 12.4 us  [on_device(): ppermute(carry_out, axis_name='chan', perm=[(dev_i, dev_i ^ ii) for dev_i...]
    all_to_all x1 -> x0, starting transfers between devices: 7.38 us -> none  [on_device(): lax.all_to_all(spectra, 'chan', split_axis=0, concat_axis=2, tiled=True)]
    convert_element_type x1 -> x0, local copies, waits for them, and re-layouts: 1.65 us -> none  [filterbank(): return spectra.astype(jnp.bfloat16)]
  transfers between devices with their start and end apart: 3 -> 9, of which waited for: 2 -> 4; matrix products, arithmetic and copies ran while one was open for 46% -> 47% of each run, Pallas kernels for 0% -> 0%
where the time goes in v1:
time: 122 us; the launch traced here: 121 us
  local copies, waits for them, and re-layouts  47.8 us (39%)
  matrix products  29.9 us (25%)
  starting transfers between devices  24.5 us (20%)
  waiting for transfers between devices  12.5 us (10%)
  other arithmetic  5.55 us (5%)
    unnamed x10, local copies, waits for them, and re-layouts  42 us
    ppermute x7, starting transfers between devices, on_device(): ppermute(carry_out, axis_name='chan', perm=[(dev_i, dev_i ^ ii) for dev_i...  17.1 us
    dot_general x1, matrix products, correlate(): jnp.einsum('ocrkaw,crkbw->ockab', stacked, right_rows, preferred_element_...  16 us
    ppermute x7, waiting for transfers between devices, on_device(): ppermute(carry_out, axis_name='chan', perm=[(dev_i, dev_i ^ ii) for dev_i...  12.4 us
    dot_general x1, matrix products, filterbank(): jnp.einsum('crsk,sitk->crit', dft_table(channels), frames, precision=lax....  7.13 us
    dot_general x1, matrix products, beamform(): jnp.einsum('scbi,crit->csrbt', weights, own_time, preferred_element_type=...  6.84 us
    all_to_all x1, starting transfers between devices, on_device(): lax.all_to_all(lax.all_to_all(beam_part, 'tile', split_axis=1, concat_axi...  3.97 us
    all_to_all x1, starting transfers between devices, on_device(): lax.all_to_all(beam_part, 'tile', split_axis=1, concat_axis=2, tiled=True)  3.43 us
  transfers between devices with their start and end apart: 9, of which 4 were waited for; matrix products, arithmetic and copies ran while one was open for 47% of the time, Pallas kernels for 0%

profile of v1, /device:TPU:0, one launch (start us, length us, event | category | flops | bytes accessed | tf_op | source)
XLA Modules:
  0.0 121.4 jit_solution(6632553230254824666)
XLA Ops:
  0.7 1.0 fusion.109
  1.6 1.7 %fusion.107 = (f32[256,1,256]{2,0,1:T(8,128)S(1)}, f32[256,1,256]{2,0,1:T(8,128)}) fusion(), kind=kLoop, calls=%fused_computation.125 | loop fusion | flops 917504 | bytes 524288 | tf_op jit(solution)/shard_map/sin | solution.py:16
  3.4 1.7 %fusion.119 = (f32[1,256]{1,0:T(1,128)S(1)}, f32[1,256]{1,0:T(1,128)S(1)}, f32[1,256]{1,0:T(1,128)S(1)}, f32[1,256]{1,0:T(1,128)S(1)}, f32[1,256]{1,0:T(1,128)},...) fusion(f32[16,256]{1,0:T(8,128)} %param.8), kind=kLoop, calls=%fused_computation.155 | loop fusion | bytes 32768 | tf_op jit(solution)/shard_map/slice | solution.py:28
  5.0 3.5 %copy.105 = bf16[2,128,5888]{1,2,0:T(8,128)(2,1)S(1)} copy(bf16[2,128,5888]{2,1,0:T(8,128)(2,1)} %param.7) | data formatting | bytes 6029312 | tf_op args[0]
  8.5 1.1 maximum_bitcast_fusion.1
  9.7 7.1 %bitcast_convert_fusion = bf16[256,2,128,8]{2,0,3,1:T(8,128)(2,1)S(1)} fusion(bf16[2,128,23,256]{1,3,2,0:T(8,128)(2,1)S(1)} %bitcast.114, f32[256,1,2,256]{3,0,2,1:T(8,128)S(1)} %get-tuple-element.30, f32[256,1,2,256]{3,0,2,1:T(8,128)S(1)} %get-tuple-element.29, f32[256]{0:T(256)} %bitcast.137, f32[256]{0:T(256)} %bitcast.138, f32[256]{0:T(256)S(1)} %bitcast.124, ...), kind=kOutput, calls=%fused_computation.10 | convolution fusion | flops 3246653440 | bytes 18890752 | tf_op jit(solution)/shard_map/crsk,sitk->crit/dot_general | solution.py:31
  16.8 0.0 copy-start.1
  16.8 0.1 constant_dynamic-slice_fusion
  17.0 6.0 %collective-permute-start.6 = (bf16[32,2,128,8]{2,0,3,1:T(8,128)(2,1)S(1)}, bf16[32,2,128,8]{2,0,3,1:T(8,128)(2,1)S(1)}, u32[]{:S(2)}, u32[]{:S(2)}) collective-permute-start(bf16[32,2,128,8]{2,0,3,1:T(8,128)(2,1)S(1)} %get-tuple-element.21), channel_id=1, source_target_pairs={{0,28},{4,24},{8,20},{12,16},{16,12},{20,8},{24,4},{28,0},{1,29},{... | collective-permute-start | bytes 393224 | tf_op jit(solution)/shard_map/ppermute | solution.py:87
  23.0 0.2 collective-permute-start.5
  23.2 0.8 collective-permute-start.4
  24.0 2.0 %collective-permute-start.3 = (bf16[32,2,128,8]{2,0,3,1:T(8,128)(2,1)S(1)}, bf16[32,2,128,8]{2,0,3,1:T(8,128)(2,1)S(1)}, u32[]{:S(2)}, u32[]{:S(2)}) collective-permute-start(bf16[32,2,128,8]{2,0,3,1:T(8,128)(2,1)S(1)} %get-tuple-element.24), channel_id=1, source_target_pairs={{0,16},{4,20},{8,24},{12,28},{16,0},{20,4},{24,8},{28,12},{1,17},{... | collective-permute-start | bytes 393224 | tf_op jit(solution)/shard_map/ppermute | solution.py:87
  26.0 1.6 %collective-permute-start = (bf16[32,2,128,8]{2,0,3,1:T(8,128)(2,1)S(1)}, bf16[32,2,128,8]{2,0,3,1:T(8,128)(2,1)S(1)}, u32[]{:S(2)}, u32[]{:S(2)}) collective-permute-start(bf16[32,2,128,8]{2,0,3,1:T(8,128)(2,1)S(1)} %get-tuple-element.27), channel_id=1, source_target_pairs={{0,4},{4,0},{8,12},{12,8},{16,20},{20,16},{24,28},{28,24},{1,5},{5... | collective-permute-start | bytes 393224 | tf_op jit(solution)/shard_map/ppermute | solution.py:87
  27.6 0.1 broadcast_in_dim.13
  27.7 0.1 copy_dynamic-update-slice_fusion.7
  27.9 0.1 copy.118
  28.1 0.1 broadcast_in_dim.22
  28.2 0.1 copy.119
  28.4 2.6 %collective-permute-done = bf16[32,2,128,8]{2,0,3,1:T(8,128)(2,1)S(1)} collective-permute-done((bf16[32,2,128,8]{2,0,3,1:T(8,128)(2,1)S(1)}, bf16[32,2,128,8]{2,0,3,1:T(8,128)(2,1)S(1)}, u32[]{:S(2)}, u32[]{:S(2)}) %collective-permute-start) | collective-permute-done | bytes 131104 | tf_op jit(solution)/shard_map/ppermute | solution.py:87
  31.0 3.5 %collective-permute-start.1 = (bf16[32,2,128,8]{2,0,3,1:T(8,128)(2,1)S(1)}, bf16[32,2,128,8]{2,0,3,1:T(8,128)(2,1)S(1)}, u32[]{:S(2)}, u32[]{:S(2)}) collective-permute-start(bf16[32,2,128,8]{2,0,3,1:T(8,128)(2,1)S(1)} %get-tuple-element.26), channel_id=1, source_target_pairs={{0,8},{4,12},{8,0},{12,4},{16,24},{20,28},{24,16},{28,20},{1,9},{5... | collective-permute-start | bytes 393224 | tf_op jit(solution)/shard_map/ppermute | solution.py:87
  34.5 0.1 copy_dynamic-update-slice_fusion.6
  34.5 2.9 %collective-permute-done.1 = bf16[32,2,128,8]{2,0,3,1:T(8,128)(2,1)S(1)} collective-permute-done((bf16[32,2,128,8]{2,0,3,1:T(8,128)(2,1)S(1)}, bf16[32,2,128,8]{2,0,3,1:T(8,128)(2,1)S(1)}, u32[]{:S(2)}, u32[]{:S(2)}) %collective-permute-start.1) | collective-permute-done | bytes 131104 | tf_op jit(solution)/shard_map/ppermute | solution.py:87
  37.4 2.9 %collective-permute-start.2 = (bf16[32,2,128,8]{2,0,3,1:T(8,128)(2,1)S(1)}, bf16[32,2,128,8]{2,0,3,1:T(8,128)(2,1)S(1)}, u32[]{:S(2)}, u32[]{:S(2)}) collective-permute-start(bf16[32,2,128,8]{2,0,3,1:T(8,128)(2,1)S(1)} %get-tuple-element.25), channel_id=1, source_target_pairs={{0,12},{4,8},{8,4},{12,0},{16,28},{20,24},{24,20},{28,16},{1,13},{... | collective-permute-start | bytes 393224 | tf_op jit(solution)/shard_map/ppermute | solution.py:87
  40.4 0.1 copy_dynamic-update-slice_fusion.5
  40.4 7.0 %collective-permute-done.2 = bf16[32,2,128,8]{2,0,3,1:T(8,128)(2,1)S(1)} collective-permute-done((bf16[32,2,128,8]{2,0,3,1:T(8,128)(2,1)S(1)}, bf16[32,2,128,8]{2,0,3,1:T(8,128)(2,1)S(1)}, u32[]{:S(2)}, u32[]{:S(2)}) %collective-permute-start.2) | collective-permute-done | bytes 131104 | tf_op jit(solution)/shard_map/ppermute | solution.py:87
  47.4 0.1 copy_dynamic-update-slice_fusion.4
  47.5 0.1 copy_dynamic-update-slice_fusion.3
  47.6 0.1 copy_dynamic-update-slice_fusion.2
  47.7 0.1 copy_dynamic-update-slice_fusion.1
  47.8 0.1 copy_dynamic-update-slice_fusion
  47.9 6.8 %fusion.58 = f32[32,2,2,64,2]{3,4,1,2,0:T(2,128)S(1)} fusion(bf16[32,2,1024,8]{2,3,1,0:T(8,128)(2,1)S(1)} %copy_dynamic-update-slice_fusion, s32[]{:T(128)S(6)} %select_n.103, bf16[2,32,64,1024]{3,2,1,0:T(8,128)(2,1)} %param.9, bf16[64,1024]{1,0:T(8,128)(2,1)S(1)} %copy.119), kind=kOutput, calls=%fused_computation.64 | convolution fusion | flops 37748736 | bytes 8847364 | tf_op jit(solution)/shard_map/scbi,crit->csrbt/dot_general | solution.py:60
  54.8 0.1 maximum_bitcast_fusion.3
  54.9 0.1 copy.123
  55.0 0.7 reshape.186
  55.7 3.4 %all-to-all-start = ((bf16[4,2,1024]{2,1,0:T(2,128)(2,1)}), bf16[4,2,1024]{2,1,0:T(2,128)(2,1)S(1)}, u32[]{:S(2)}, u32[]{:S(2)}) async-start(bf16[4,2,1024]{2,1,0:T(2,128)(2,1)} %reshape.186), calls=%async_computation | async-start | bytes 32768 | tf_op jit(solution)/shard_map/all_to_all | solution.py:99
  59.1 1.0 gather_fusion.1
  60.1 1.2 %fusion.97 = (bf16[1,32,2,9,128,8]{4,5,2,0,3,1:T(8,128)(2,1)}, bf16[32,2,9,128,8]{3,4,1,2,0:T(8,128)(2,1)S(1)}) fusion(bf16[9,32,2,128,8]{3,4,2,1,0:T(8,128)(2,1)S(1)} %gather_fusion.1, pred[9]{0:T(512)(128)(4,1)S(1)} %get-tuple-element.47), kind=kLoop, calls=%fused_computation.107 | loop fusion | flops 589824 | bytes 3538953 | tf_op jit(solution)/shard_map/stack | solution.py:49
  61.4 0.2 fusion.118
  61.5 0.2 maximum_bitcast_fusion
  61.7 1.0 gather_fusion
  62.7 0.1 all-to-all-done
  62.8 0.1 reshape.187
  62.9 0.7 reshape.188
  63.7 4.0 %all-to-all-start.1 = ((bf16[8,2,512]{2,1,0:T(2,128)(2,1)}), bf16[8,2,512]{2,1,0:T(2,128)(2,1)S(1)}, u32[]{:S(2)}, u32[]{:S(2)}) async-start(bf16[8,2,512]{2,1,0:T(2,128)(2,1)} %reshape.188), calls=%async_computation.1 | async-start | bytes 32768 | tf_op jit(solution)/shard_map/all_to_all | solution.py:98
  67.6 16.0 %fusion = f32[2,32,9,128,128]{3,4,0,2,1:T(8,128)} fusion(bf16[1,32,2,9,128,8]{4,5,2,0,3,1:T(8,128)(2,1)S(1)} %maximum_bitcast_fusion, bf16[1,32,2,9,128,8]{4,5,2,0,3,1:T(8,128)(2,1)} %get-tuple-element.17, bf16[9,32,2,128,8]{3,4,2,1,0:T(8,128)(2,1)S(1)} %gather_fusion, pred[9]{0:T(512)(128)(4,1)S(1)} %get-tuple-element.13), kind=kOutput, calls=%fused_computation.3 | convolution fusion | flops 316735488 | bytes 41287688 | tf_op jit(solution)/shard_map/ocrkaw,crkbw->ockab/dot_general | solution.py:50
  83.6 36.9 %copy.128 = f32[2,32,9,128,128]{4,3,2,1,0:T(8,128)} copy(f32[2,32,9,128,128]{3,4,0,2,1:T(8,128)} %fusion) | data formatting | bytes 75497472
  120.5 0.1 reshape.189
  120.6 0.7 all_to_all.27
  (17 shorter events, 0.2 us)
Async XLA Ops:
  16.8 11.0 %copy-start.1 = (s32[9,2]{0,1:T(2,128)S(1)}, s32[9,2]{0,1:T(2,128)}, u32[]{:S(2)}) copy-start(s32[9,2]{0,1:T(2,128)} %param.11) | copy-start | bytes 220
  16.8 11.1 %copy-start = (s32[64,512]{1,0:T(8,128)S(1)}, s32[64,512]{1,0:T(8,128)}, u32[]{:S(2)}) copy-start(s32[64,512]{1,0:T(8,128)} %param.10) | copy-start | bytes 393220
  17.0 30.8 %collective-permute-start.6 = (bf16[32,2,128,8]{2,0,3,1:T(8,128)(2,1)S(1)}, bf16[32,2,128,8]{2,0,3,1:T(8,128)(2,1)S(1)}, u32[]{:S(2)}, u32[]{:S(2)}) collective-permute-start(bf16[32,2,128,8]{2,0,3,1:T(8,128)(2,1)S(1)} %get-tuple-element.21), channel_id=1, source_target_pairs={{0,28},{4,24},{8,20},{12,16},{16,12},{20,8},{24,4},{28,0},{1,29},{... | collective-permute-start | bytes 393224 | tf_op jit(solution)/shard_map/ppermute | solution.py:87
  23.0 24.7 %collective-permute-start.5 = (bf16[32,2,128,8]{2,0,3,1:T(8,128)(2,1)S(1)}, bf16[32,2,128,8]{2,0,3,1:T(8,128)(2,1)S(1)}, u32[]{:S(2)}, u32[]{:S(2)}) collective-permute-start(bf16[32,2,128,8]{2,0,3,1:T(8,128)(2,1)S(1)} %get-tuple-element.22), channel_id=1, source_target_pairs={{0,24},{4,28},{8,16},{12,20},{16,8},{20,12},{24,0},{28,4},{1,25},{... | collective-permute-start | bytes 393224 | tf_op jit(solution)/shard_map/ppermute | solution.py:87
  23.2 24.4 %collective-permute-start.4 = (bf16[32,2,128,8]{2,0,3,1:T(8,128)(2,1)S(1)}, bf16[32,2,128,8]{2,0,3,1:T(8,128)(2,1)S(1)}, u32[]{:S(2)}, u32[]{:S(2)}) collective-permute-start(bf16[32,2,128,8]{2,0,3,1:T(8,128)(2,1)S(1)} %get-tuple-element.23), channel_id=1, source_target_pairs={{0,20},{4,16},{8,28},{12,24},{16,4},{20,0},{24,12},{28,8},{1,21},{... | collective-permute-start | bytes 393224 | tf_op jit(solution)/shard_map/ppermute | solution.py:87
  24.0 23.5 %collective-permute-start.3 = (bf16[32,2,128,8]{2,0,3,1:T(8,128)(2,1)S(1)}, bf16[32,2,128,8]{2,0,3,1:T(8,128)(2,1)S(1)}, u32[]{:S(2)}, u32[]{:S(2)}) collective-permute-start(bf16[32,2,128,8]{2,0,3,1:T(8,128)(2,1)S(1)} %get-tuple-element.24), channel_id=1, source_target_pairs={{0,16},{4,20},{8,24},{12,28},{16,0},{20,4},{24,8},{28,12},{1,17},{... | collective-permute-start | bytes 393224 | tf_op jit(solution)/shard_map/ppermute | solution.py:87
  26.0 5.0 %collective-permute-start = (bf16[32,2,128,8]{2,0,3,1:T(8,128)(2,1)S(1)}, bf16[32,2,128,8]{2,0,3,1:T(8,128)(2,1)S(1)}, u32[]{:S(2)}, u32[]{:S(2)}) collective-permute-start(bf16[32,2,128,8]{2,0,3,1:T(8,128)(2,1)S(1)} %get-tuple-element.27), channel_id=1, source_target_pairs={{0,4},{4,0},{8,12},{12,8},{16,20},{20,16},{24,28},{28,24},{1,5},{5... | collective-permute-start | bytes 393224 | tf_op jit(solution)/shard_map/ppermute | solution.py:87
  31.0 6.4 %collective-permute-start.1 = (bf16[32,2,128,8]{2,0,3,1:T(8,128)(2,1)S(1)}, bf16[32,2,128,8]{2,0,3,1:T(8,128)(2,1)S(1)}, u32[]{:S(2)}, u32[]{:S(2)}) collective-permute-start(bf16[32,2,128,8]{2,0,3,1:T(8,128)(2,1)S(1)} %get-tuple-element.26), channel_id=1, source_target_pairs={{0,8},{4,12},{8,0},{12,4},{16,24},{20,28},{24,16},{28,20},{1,9},{5... | collective-permute-start | bytes 393224 | tf_op jit(solution)/shard_map/ppermute | solution.py:87
  37.4 10.0 %collective-permute-start.2 = (bf16[32,2,128,8]{2,0,3,1:T(8,128)(2,1)S(1)}, bf16[32,2,128,8]{2,0,3,1:T(8,128)(2,1)S(1)}, u32[]{:S(2)}, u32[]{:S(2)}) collective-permute-start(bf16[32,2,128,8]{2,0,3,1:T(8,128)(2,1)S(1)} %get-tuple-element.25), channel_id=1, source_target_pairs={{0,12},{4,8},{8,4},{12,0},{16,28},{20,24},{24,20},{28,16},{1,13},{... | collective-permute-start | bytes 393224 | tf_op jit(solution)/shard_map/ppermute | solution.py:87
  55.7 7.1 %all-to-all-start = ((bf16[4,2,1024]{2,1,0:T(2,128)(2,1)}), bf16[4,2,1024]{2,1,0:T(2,128)(2,1)S(1)}, u32[]{:S(2)}, u32[]{:S(2)}) async-start(bf16[4,2,1024]{2,1,0:T(2,128)(2,1)} %reshape.186), calls=%async_computation | async-start | bytes 32768 | tf_op jit(solution)/shard_map/all_to_all | solution.py:99
  63.7 56.8 %all-to-all-start.1 = ((bf16[8,2,512]{2,1,0:T(2,128)(2,1)}), bf16[8,2,512]{2,1,0:T(2,128)(2,1)S(1)}, u32[]{:S(2)}, u32[]{:S(2)}) async-start(bf16[8,2,512]{2,1,0:T(2,128)(2,1)} %reshape.188), calls=%async_computation.1 | async-start | bytes 32768 | tf_op jit(solution)/shard_map/all_to_all | solution.py:98
